TPU v7x, 128 devices: a whole 4x4x4 slice. The times are simulated.
128 devices in a mesh: dp: 16 (over x, y), expert: 8 (over z, core).
Axes of the slice: x: 4, y: 4, z: 4, core: 2. Of those that a mesh axis runs over, the one named last changes fastest.
Arguments:
- hidden: bfloat16 [16384, 2, 7168], P(('dp', 'expert')), may hold values from -6 to 6
- grad_out: bfloat16 [16384, 2048], P(('dp', 'expert')), may hold values from -6 to 6
- gate_weights: float32 [16384, 2], P(('dp', 'expert')), may hold values from 0.1 to 1
- routes: int32 [16384, 2], P(('dp', 'expert')), may hold values from 0 to 7, all different within a row; in each aligned block of 128 rows (0 to 127, 128 to 255, ...) at most 48 rows name the same one
- example_ids: int32 [16384], P(('dp', 'expert')), may hold values from 0 to 127, as said below
Outputs:
- update: bfloat16 [8, 7168, 2048], P('expert', 'dp')
- norm_ratio: float32 [128], P('dp')
Inputs may be any that keep to these rules, and one draw needn't show every extreme that they name: `routes`: among the 128 tokens of one device no expert is named by more than 48 tokens, and some device reaches 48 for some expert. `example_ids`: ids never fall along the tokens; tokens i * 1024 to (i + 1) * 1024 - 1 hold exactly the examples i * 8 to (i + 1) * 8 - 1, each with one or more tokens.
All inputs are finite; a program needn't handle non-finite values.
Results may differ from a plain program's by a relative error of at most 0.019.
Values may be sent and summed in bfloat16 or wider, within the bound.
A program may use at most 128 MiB of HBM per device.

v0:
```python
import math

import jax
import jax.numpy as jnp
from jax import lax
from jax.sharding import PartitionSpec as P

EX_BLK = 8


def body(hidden, grad_out, gate_weights, routes, example_ids):
    experts = lax.axis_size("expert")
    replicas = lax.axis_size("dp")
    replica = lax.axis_index("dp")
    tokens_here = hidden.shape[0]
    hidden_width = hidden.shape[2]
    out_width = grad_out.shape[1]
    capacity = 3 * tokens_here // experts
    row_count = experts * capacity
    examples = EX_BLK * replicas
    threshold = math.sqrt(hidden_width * out_width * tokens_here * (0.43 + 0.01 * tokens_here))
    grad_rows = (gate_weights[:, :, None] * grad_out[:, None, :].astype(jnp.float32)).astype(
        jnp.bfloat16
    )
    route_flat = routes.reshape(-1)
    chosen = (route_flat[:, None] == jnp.arange(experts, dtype=jnp.int32)[None, :]).astype(
        jnp.int32
    )
    position = jnp.sum((jnp.cumsum(chosen, axis=0) - 1) * chosen, axis=1)
    destin = route_flat * capacity + position
    hidden_sent = (
        jnp.zeros((experts * capacity, hidden_width), jnp.bfloat16)
        .at[destin]
        .set(hidden.reshape(-1, hidden_width))
    )
    grads_sent = (
        jnp.zeros((experts * capacity, out_width), jnp.bfloat16)
        .at[destin]
        .set(grad_rows.reshape(-1, out_width))
    )
    owner_sent = (
        jnp.full((experts * capacity,), -1, jnp.int32).at[destin].set(jnp.repeat(example_ids, 2))
    )
    hidden_in, grads_in, owner_in = (
        lax.all_to_all(
            hidden_sent.reshape(experts, capacity, hidden_width),
            "expert",
            split_axis=0,
            concat_axis=0,
            tiled=True,
        ),
        lax.all_to_all(
            grads_sent.reshape(experts, capacity, out_width),
            "expert",
            split_axis=0,
            concat_axis=0,
            tiled=True,
        ),
        lax.all_to_all(
            owner_sent.reshape(experts, capacity), "expert", split_axis=0, concat_axis=0, tiled=True
        ),
    )
    hidden_in = hidden_in.reshape(row_count, hidden_width)
    grads_in = grads_in.reshape(row_count, out_width)
    owner_in = owner_in.reshape(row_count)
    first_example = replica * EX_BLK
    belongs = (
        owner_in[:, None] == first_example + jnp.arange(EX_BLK, dtype=jnp.int32)[None, :]
    ).astype(jnp.float32)
    hidden_gram = jnp.dot(hidden_in, hidden_in.T, preferred_element_type=jnp.float32)
    grad_gram = jnp.dot(grads_in, grads_in.T, preferred_element_type=jnp.float32)
    matched = (owner_in[:, None] == owner_in[None, :]).astype(jnp.float32)
    row_sums = jnp.sum(hidden_gram * grad_gram * matched, axis=1)
    square_part = jnp.sum(row_sums[:, None] * belongs, axis=0)
    squares = lax.psum(square_part, "expert")
    norm_values = jnp.sqrt(squares)
    factors = jnp.minimum(1.0, threshold / norm_values)
    row_factors = jnp.sum(belongs * factors[None, :], axis=1)
    clipped = (row_factors[:, None] * grads_in.astype(jnp.float32)).astype(jnp.bfloat16)
    shard_width = hidden_width // replicas
    reduced = lax.psum_scatter(
        lax.dot_general(
            hidden_in, clipped, (((0,), (0,)), ((), ())), preferred_element_type=jnp.float32
        ).astype(jnp.bfloat16),
        "dp",
        scatter_dimension=0,
        tiled=True,
    ).astype(jnp.float32)
    update = (reduced / examples).astype(jnp.bfloat16).reshape(1, shard_width, out_width)
    return (update, norm_values / threshold)


def solution(mesh):
    return jax.shard_map(
        body,
        mesh=mesh,
        in_specs=(
            P(("dp", "expert"), None, None),
            P(("dp", "expert"), None),
            P(("dp", "expert"), None),
            P(("dp", "expert"), None),
            P(("dp", "expert")),
        ),
        out_specs=(P("expert", "dp", None), P("dp")),
        check_vma=False,
    )
```

profile of v0, /device:TPU:1, one launch (start us, length us, event | category | flops | bytes accessed | tf_op | source)
XLA Modules:
  0.0 352.0 jit_solution(234594148419169205)
XLA Ops:
  7.2 0.7 broadcast_multiply_fusion
  7.8 0.8 copy.12
  8.6 0.1 eq.57
  8.8 0.1 eq.53
  8.9 0.1 copy.11
  9.0 0.1 mul.75
  9.2 0.6 reduce-window.6
  9.8 0.2 slice_reduce_fusion
  10.0 0.7 broadcast_in_dim.10
  10.8 0.1 reshape.122
  10.9 0.1 fusion.11
  11.0 1.4 scatter_custom_fusion.1
  12.4 0.7 all_to_all.13
  13.1 6.8 %all-to-all-start.1 = ((s32[8,1,48]{2,1,0:T(1,128)}), s32[8,1,48]{2,1,0:T(1,128)S(1)}, u32[]{:S(2)}, u32[]{:S(2)}) async-start(s32[8,1,48]{2,1,0:T(1,128)} %all_to_all.13), calls=%async_computation.1 | async-start | bytes 8192 | tf_op jit(solution)/shard_map/all_to_all | solution.py:59
  19.9 8.4 %reshape.114 = bf16[256,7168]{1,0:T(8,128)(2,1)} reshape(bf16[128,2,7168]{2,1,0:T(2,128)(2,1)} %param.5) | data formatting | bytes 7340032 | tf_op jit(solution)/shard_map/reshape | solution.py:34
  28.3 10.1 %scatter_custom_fusion = bf16[384,7168]{1,0:T(8,128)(2,1)} fusion(s32[256]{0:T(256)S(1)} %bitcast.28, bf16[256,7168]{1,0:T(8,128)(2,1)} %reshape.114, bf16[]{:T(256)} %constant.13.clone.1), kind=kCustom, calls=%fused_computation.6 | custom fusion | bytes 5505536 | tf_op jit(solution)/shard_map/scatter | solution.py:34
  38.4 0.0 all-to-all-done.1
  38.4 0.0 copy-start.1
  38.4 0.0 copy-start
  38.4 4.9 %all-to-all-start = ((bf16[8,48,7168]{2,1,0:T(8,128)(2,1)}), bf16[8,48,7168]{2,1,0:T(8,128)(2,1)}, u32[]{:S(2)}, u32[]{:S(2)}) async-start(bf16[8,48,7168]{2,1,0:T(8,128)(2,1)} %bitcast.24), calls=%async_computation | async-start | bytes 11010048 | tf_op jit(solution)/shard_map/all_to_all | solution.py:45
  43.3 0.0 copy-done.1
  43.3 0.1 copy.14
  43.5 0.1 mul.78
  43.6 0.0 copy-done
  43.6 1.0 mul.80
  44.7 2.5 mul.81
  47.1 4.5 %scatter_custom_fusion.2 = bf16[384,2048]{1,0:T(8,128)(2,1)} fusion(s32[256]{0:T(256)S(1)} %bitcast.29, f32[256,2048]{1,0:T(8,128)} %mul.81, f32[256]{0:T(256)S(1)} %mul.78, bf16[]{:T(256)} %constant.13.clone.1), kind=kCustom, calls=%fused_computation.14 | custom fusion | flops 1048576 | bytes 3671042 | tf_op jit(solution)/shard_map/scatter | solution.py:39
  51.7 54.6 %all-to-all-done = bf16[8,48,7168]{2,1,0:T(8,128)(2,1)} async-done(((bf16[8,48,7168]{2,1,0:T(8,128)(2,1)}), bf16[8,48,7168]{2,1,0:T(8,128)(2,1)}, u32[]{:S(2)}, u32[]{:S(2)}) %all-to-all-start) | async-done | bytes 5505056 | tf_op jit(solution)/shard_map/all_to_all | solution.py:45
  106.3 4.4 %all-to-all-start.2 = ((bf16[8,48,2048]{2,1,0:T(8,128)(2,1)}), bf16[8,48,2048]{2,1,0:T(8,128)(2,1)S(1)}, u32[]{:S(2)}, u32[]{:S(2)}) async-start(bf16[8,48,2048]{2,1,0:T(8,128)(2,1)} %bitcast.6), calls=%async_computation.2 | async-start | bytes 3145728 | tf_op jit(solution)/shard_map/all_to_all | solution.py:52
  110.6 0.0 reduce-scatter.2.cloned.1.call-start
  110.6 0.5 broadcast.104
  111.1 0.7 reduce.5
  111.8 0.1 eq.61
  111.9 8.1 %fusion.15 = f32[384,384]{0,1:T(8,128)S(1)} fusion(bf16[384,7168]{1,0:T(8,128)(2,1)} %bitcast.5), kind=kOutput, calls=%fused_computation.34 | convolution fusion | flops 2113929216 | bytes 6094848 | tf_op jit(solution)/shard_map/dot_general | solution.py:70
  120.0 11.3 %all-to-all-done.2 = bf16[8,48,2048]{2,1,0:T(8,128)(2,1)S(1)} async-done(((bf16[8,48,2048]{2,1,0:T(8,128)(2,1)}), bf16[8,48,2048]{2,1,0:T(8,128)(2,1)S(1)}, u32[]{:S(2)}, u32[]{:S(2)}) %all-to-all-start.2) | async-done | bytes 1572896 | tf_op jit(solution)/shard_map/all_to_all | solution.py:52
  131.4 1.0 fusion.5
  132.4 0.2 fusion.9
  132.6 12.6 %psum.7 = f32[8]{0:T(128)S(1)} all-reduce(f32[8]{0:T(128)S(1)} %fusion.9), channel_id=1, replica_groups=mesh['dp'=16,'expert'=8] {'expert'}, use_global_device_ids=true, to_apply=%region_8.9 | all-reduce | flops 8 | bytes 64 | tf_op jit(solution)/shard_map/psum | solution.py:75
  145.2 0.5 sqrt_multiply_fusion
  145.7 0.1 fusion.10
  145.8 0.1 mul.89
  145.9 22.0 %bitcast_convert_fusion = bf16[7168,2048]{1,0:T(8,128)(2,1)} fusion(bf16[8,48,7168]{2,1,0:T(8,128)(2,1)} %all-to-all-done, bf16[8,48,2048]{2,1,0:T(8,128)(2,1)S(1)} %all-to-all-done.2, f32[8,48]{1,0:T(8,128)S(1)} %mul.89), kind=kOutput, calls=%fused_computation.3 | convolution fusion | flops 11291328512 | bytes 36439552 | tf_op jit(solution)/shard_map/dot_general | solution.py:82
  167.8 0.0 reduce-scatter.2.cloned.1.call-update
  167.9 174.1 %reduce-scatter.2.cloned.1.call-done = bf16[448,2048]{1,0:T(8,128)(2,1)} async-done(((bf16[7168,2048]{1,0:T(8,128)(2,1)}), bf16[448,2048]{1,0:T(8,128)(2,1)}) %reduce-scatter.2.cloned.1.call-update) | async-done | bytes 1835024 | tf_op jit(solution)/shard_map/reduce_scatter | solution.py:81
  341.9 3.2 fusion.2
  (5 shorter events, 0.1 us)
Async XLA Ops:
  13.1 25.3 %all-to-all-start.1 = ((s32[8,1,48]{2,1,0:T(1,128)}), s32[8,1,48]{2,1,0:T(1,128)S(1)}, u32[]{:S(2)}, u32[]{:S(2)}) async-start(s32[8,1,48]{2,1,0:T(1,128)} %all_to_all.13), calls=%async_computation.1 | async-start | bytes 8192 | tf_op jit(solution)/shard_map/all_to_all | solution.py:59
  38.4 5.0 %copy-start.1 = (f32[128,2]{0,1:T(2,128)S(1)}, f32[128,2]{0,1:T(2,128)}, u32[]{:S(2)}) copy-start(f32[128,2]{0,1:T(2,128)} %param.7) | copy-start | bytes 3076
  38.4 5.2 %copy-start = (bf16[128,2048]{1,0:T(8,128)(2,1)S(1)}, bf16[128,2048]{1,0:T(8,128)(2,1)}, u32[]{:S(2)}) copy-start(bf16[128,2048]{1,0:T(8,128)(2,1)} %param.6) | copy-start | bytes 1572868
  38.4 67.9 %all-to-all-start = ((bf16[8,48,7168]{2,1,0:T(8,128)(2,1)}), bf16[8,48,7168]{2,1,0:T(8,128)(2,1)}, u32[]{:S(2)}, u32[]{:S(2)}) async-start(bf16[8,48,7168]{2,1,0:T(8,128)(2,1)} %bitcast.24), calls=%async_computation | async-start | bytes 11010048 | tf_op jit(solution)/shard_map/all_to_all | solution.py:45
  106.3 25.1 %all-to-all-start.2 = ((bf16[8,48,2048]{2,1,0:T(8,128)(2,1)}), bf16[8,48,2048]{2,1,0:T(8,128)(2,1)S(1)}, u32[]{:S(2)}, u32[]{:S(2)}) async-start(bf16[8,48,2048]{2,1,0:T(8,128)(2,1)} %bitcast.6), calls=%async_computation.2 | async-start | bytes 3145728 | tf_op jit(solution)/shard_map/all_to_all | solution.py:52
  110.6 231.3 %reduce-scatter.2.cloned.1.call-start = ((), (), s32[]{:S(2)}) async-start(), calls=%async_computation.4 | async-start | bytes 31195136 | tf_op jit(solution)/shard_map/reduce_scatter | solution.py:81
Sparse Core Ops, SparseCore 0:
  168.0 173.8 reduce-scatter.1
where the time goes:
time: 353 us; the launch traced here: 352 us
  waiting for transfers between devices  240 us (68%)
  matrix products  31.1 us (9%)
  local copies, waits for them, and re-layouts  27.4 us (8%)
  starting transfers between devices  16.1 us (5%)
  between operations  14.1 us (4%)
  blocking collectives  12.6 us (4%)
  other arithmetic  10.6 us (3%)
    reduce_scatter x1, waiting for transfers between devices, body(): lax.psum_scatter(lax.dot_general(hidden_in, clipped, (((0,), (0,)), ((),...  174 us
    all_to_all x1, waiting for transfers between devices, body(): lax.all_to_all(hidden_sent.reshape(experts, capacity, hidden_width), 'exp...  54.6 us
    dot_general x1, matrix products, body(): lax.dot_general(hidden_in, clipped, (((0,), (0,)), ((), ())), preferred_e...  22 us
    psum x1, blocking collectives, body(): squares = lax.psum(square_part, 'expert')  12.6 us
    all_to_all x1, waiting for transfers between devices, body(): lax.all_to_all(grads_sent.reshape(experts, capacity, out_width), 'expert'...  11.3 us
    scatter x1, local copies, waits for them, and re-layouts, body(): hidden_sent = jnp.zeros((experts * capacity, hidden_width), jnp.bfloat16)...  10.1 us
    reshape x1, local copies, waits for them, and re-layouts, body(): hidden.reshape(-1, hidden_width)  8.4 us
    dot_general x1, matrix products, body(): jnp.dot(hidden_in, hidden_in.T, preferred_element_type=jnp.float32)  8.14 us
  transfers between devices with their start and end apart: 4, of which 3 were waited for; matrix products, arithmetic and copies ran while one was open for 10% of the time, Pallas kernels for 0%

commit v1 on v0

v1 whole, which is shorter than its diff:
```python
import math

import jax
import jax.numpy as jnp
from jax import lax
from jax.experimental import pallas as pl
from jax.experimental.pallas import tpu as pltpu
from jax.sharding import PartitionSpec as P

MESH = pl.DeviceIdType.MESH
BF16, F32 = jnp.bfloat16, jnp.float32

SIDE = 4
EXPERTS = 8
EX_BLK = 8
LANES = 128
TILE = 512


def _dot(a, b):
    return lax.dot_general(a, b, (((1,), (0,)), ((), ())), preferred_element_type=F32)


def _dot_t(a, b):
    return lax.dot_general(a, b, (((1,), (1,)), ((), ())), preferred_element_type=F32)


def kernel(
    small, hid, grad, out, norm_out,
    hv, hp, gv, gs, hs, gall, hin, hg, ht, oh, hgram, mgram, rowf,
    sq_send, sq_recv, f_send, f_recv, part_a, part_b, part_c, part_in, own,
    in_sem, z_send, z_recv, fg_send, fg_recv, fh_send, fh_recv,
    sq_ssem, sq_rsem, f_ssem, f_rsem, rs_send, rs_recv,
):
    tokens, _, width = hid.shape
    out_width = grad.shape[1]
    cap = 3 * tokens // EXPERTS
    rows = EXPERTS * cap
    half = rows // 2
    slice_w = width // SIDE
    chunk = slice_w // SIDE
    hc = chunk // 2
    threshold = math.sqrt(width * out_width * tokens * (0.43 + 0.01 * tokens))

    dp, ex = lax.axis_index("dp"), lax.axis_index("expert")
    x, y = lax.div(dp, SIDE), lax.rem(dp, SIDE)
    z, c = lax.div(ex, 2), lax.rem(ex, 2)
    gpos = y + c * (x - y)
    rpos = x + c * (y - x)

    def along(d, turned):
        a = x * SIDE + lax.rem(y + d, SIDE)
        b = lax.rem(x + d, SIDE) * SIDE + y
        return (a + turned * (b - a), ex)

    def gather_peer(d):
        return along(d, c)

    def sum_peer(d):
        return along(d, 1 - c)

    zsteps = [(2, 0), (2, 1), (1, 0), (3, 0), (1, 1), (3, 1), (0, 1)]

    def z_peer(dz, dc):
        pz = lax.rem(z + dz, SIDE)
        pc = c if dc == 0 else 1 - c
        return pz, pc

    g_in = pltpu.make_async_copy(grad, gv, in_sem.at[0])
    h_in = pltpu.make_async_copy(hid, hv, in_sem.at[1])
    g_in.start()
    h_in.start()

    barrier = pltpu.get_barrier_semaphore()
    peers = []
    for dz, dc in zsteps:
        pz, pc = z_peer(dz, dc)
        peers.append((dp, pz * 2 + pc))
    for d in (1, 2, 3):
        peers.append(gather_peer(d))
    for d in (1, 3):
        peers.append(sum_peer(d))
    for peer in peers:
        pl.semaphore_signal(barrier, inc=1, device_id=peer, device_id_type=MESH)

    pairs = 2 * tokens
    route = small[0:1, :]
    gate = small[1:2, :]
    local_id = small[2:3, :] - (dp * EX_BLK).astype(F32)
    expert_of = lax.broadcasted_iota(jnp.int32, (EXPERTS, pairs), 0)
    chosen = route == expert_of.astype(F32)
    before = lax.broadcasted_iota(jnp.int32, (pairs, pairs), 0) < lax.broadcasted_iota(
        jnp.int32, (pairs, pairs), 1
    )
    place = _dot(
        jnp.where(chosen, 1.0, 0.0).astype(BF16), jnp.where(before, 1.0, 0.0).astype(BF16)
    )
    base = (lax.rem(expert_of, 2) * half + lax.div(expert_of, 2) * cap).astype(F32)
    slot = jnp.sum(jnp.where(chosen, base + place, 0.0), axis=0, keepdims=True)
    hit = slot == lax.broadcasted_iota(jnp.int32, (rows, pairs), 0).astype(F32)
    onehot = jnp.where(hit, 1.0, 0.0).astype(BF16)
    oh[...] = onehot
    to_token = jnp.where(
        lax.div(lax.broadcasted_iota(jnp.int32, (pairs, tokens), 0), 2)
        == lax.broadcasted_iota(jnp.int32, (pairs, tokens), 1),
        1.0,
        0.0,
    ).astype(BF16)
    token_hot = _dot(onehot, to_token).astype(BF16)
    slot_gate = jnp.sum(jnp.where(hit, gate, 0.0), axis=1, keepdims=True)
    slot_id = jnp.sum(jnp.where(hit, local_id + 1.0, 0.0), axis=1, keepdims=True) - 1.0
    lane = lax.broadcasted_iota(jnp.int32, (rows, LANES), 1).astype(F32)
    gs[:, out_width:] = jnp.where(slot_id == lane, 1.0, 0.0).astype(BF16)
    g_in.wait()
    for n in range(out_width // TILE):
        cols = slice(n * TILE, (n + 1) * TILE)
        gs[:, cols] = (slot_gate * _dot(token_hot, gv[:, cols])).astype(BF16)

    pl.semaphore_wait(barrier, len(peers))

    my_rows = pl.ds(pl.multiple_of(ex * cap, 16), cap)
    my_grad_rows = pl.ds(pl.multiple_of(3 * rows + ex * cap, 16), cap)

    def block(pz, pc):
        return pl.ds(pl.multiple_of(pc * half + pz * cap, 16), cap)

    def z_copies(k):
        copies = []
        for i, (dz, dc) in enumerate(zsteps):
            pz, pc = z_peer(dz, dc)
            if k == 0:
                src, dst = gs.at[block(pz, pc)], gall.at[my_grad_rows]
            else:
                src, dst = hs.at[k - 1, block(pz, pc)], hin.at[k - 1, my_rows]
            copies.append(
                pltpu.make_async_remote_copy(
                    src_ref=src,
                    dst_ref=dst,
                    send_sem=z_send.at[k, i],
                    recv_sem=z_recv.at[k, i],
                    device_id=(dp, pz * 2 + pc),
                    device_id_type=MESH,
                )
            )
        return copies

    zc = [z_copies(k) for k in range(1 + SIDE)]
    for copy in zc[0]:
        copy.start()
    gall[my_grad_rows, :] = gs[block(z, c), :]

    h_in.wait()
    for j in range(SIDE):
        for a in range(SIDE // 2):
            first, second = (2 * a * SIDE + j) * chunk, ((2 * a + 1) * SIDE + j) * chunk
            pair = jnp.concatenate(
                [
                    hv[:, :, first : first + chunk].reshape(pairs, chunk),
                    hv[:, :, second : second + chunk].reshape(pairs, chunk),
                ],
                axis=1,
            )
            at = j * slice_w + 2 * a * chunk
            hp[:, at : at + 2 * chunk] = pair

    def pack(q):
        je = pl.ds(pl.multiple_of(lax.rem(y + 1 + q, SIDE) * slice_w, LANES), slice_w)
        jo = pl.ds(pl.multiple_of(lax.rem(x + 1 + q, SIDE) * slice_w, LANES), slice_w)
        hs[q, 0:half, :] = _dot(oh[0:half, :], hp[:, je]).astype(BF16)
        hs[q, half:rows, :] = _dot(
            oh[half:rows, :], hv[:, :, jo].reshape(pairs, slice_w)
        ).astype(BF16)

    def forward_grads(d):
        return pltpu.make_async_remote_copy(
            src_ref=gall.at[3 * rows : 4 * rows],
            dst_ref=gall.at[(d - 1) * rows : d * rows],
            send_sem=fg_send.at[d - 1],
            recv_sem=fg_recv.at[d - 1],
            device_id=gather_peer(d),
            device_id_type=MESH,
        )

    def forward_hidden(q):
        return pltpu.make_async_remote_copy(
            src_ref=hin.at[q],
            dst_ref=hg.at[q],
            send_sem=fh_send.at[q],
            recv_sem=fh_recv.at[q],
            device_id=gather_peer(q + 1),
            device_id_type=MESH,
        )

    fgs = [forward_grads(d) for d in (1, 2, 3)]
    fhs = [forward_hidden(q) for q in range(SIDE - 1)]

    for k in range(1 + SIDE):
        if k < SIDE:
            pack(k)
            for copy in zc[k + 1]:
                copy.start()
            hin[k, my_rows, :] = hs[k, block(z, c), :]
        for copy in zc[k]:
            copy.wait_recv()
        if k == 0:
            for copy in fgs:
                copy.start()
            g = gall[3 * rows : 4 * rows, 0:out_width]
            b = gall[3 * rows : 4 * rows, out_width:]
            mgram[...] = _dot_t(g, g) * _dot_t(b, b)
        else:
            if k < SIDE:
                fhs[k - 1].start()
            h = hin[k - 1]
            gram = _dot_t(h, h)
            if k > 1:
                gram = gram + hgram[...]
            if k < SIDE:
                hgram[...] = gram
            else:
                row_sums = jnp.sum(gram * mgram[...], axis=1, keepdims=True)
                member = gall[3 * rows : 4 * rows, out_width:].astype(F32)
                part = jnp.sum(row_sums * member, axis=0, keepdims=True)
                sq_send[...] = jnp.broadcast_to(part, (8, LANES))

    sq_copies = []
    for i, (dz, dc) in enumerate(zsteps):
        pz, pc = z_peer(dz, dc)
        sq_copies.append(
            pltpu.make_async_remote_copy(
                src_ref=sq_send,
                dst_ref=sq_recv.at[i],
                send_sem=sq_ssem.at[i],
                recv_sem=sq_rsem.at[i],
                device_id=(dp, pz * 2 + pc),
                device_id_type=MESH,
            )
        )
    for copy in sq_copies:
        copy.start()
    ht[:, 3 * rows : 4 * rows] = hin[SIDE - 1].T
    total = sq_send[...]
    for i, copy in enumerate(sq_copies):
        copy.wait_recv()
        total = total + sq_recv[i]
    norms = jnp.sqrt(total)
    norm_out[...] = norms[0:1, 0:EX_BLK] / threshold
    f_send[...] = jnp.minimum(1.0, threshold / norms)
    f_copies = []
    for d in (1, 2, 3):
        f_copies.append(
            pltpu.make_async_remote_copy(
                src_ref=f_send,
                dst_ref=f_recv.at[d - 1],
                send_sem=f_ssem.at[d - 1],
                recv_sem=f_rsem.at[d - 1],
                device_id=gather_peer(d),
                device_id_type=MESH,
            )
        )
    for copy in f_copies:
        copy.start()
    for q in range(SIDE - 1):
        fhs[q].wait_recv()
        ht[:, q * rows : (q + 1) * rows] = hg[q].T
    for copy in fgs:
        copy.wait_recv()
        copy.wait_send()
    for copy in f_copies:
        copy.wait_recv()
    for q in range(SIDE):
        span = slice(q * rows, (q + 1) * rows)
        factors = f_send[0:1, :] if q == SIDE - 1 else f_recv[q, 0:1, :]
        row_factor = jnp.sum(
            gall[span, out_width:].astype(F32) * factors, axis=1, keepdims=True
        )
        rowf[span, :] = jnp.broadcast_to(row_factor, (rows, LANES))

    def chunk_rows(d, lower, size):
        start = lax.rem(rpos + d, SIDE) * chunk + lower * hc
        return pl.ds(pl.multiple_of(start, 32), size)

    def tile_at(n):
        return pl.ds(pl.multiple_of(n * TILE, TILE), TILE)

    def rs_copy(slot_, n):
        src = (
            part_a.at[0:hc],
            part_b.at[0],
            part_c.at[0],
            part_a.at[hc:chunk],
            part_b.at[1],
            part_c.at[1],
        )[slot_]
        return pltpu.make_async_remote_copy(
            src_ref=src.at[:, tile_at(n)],
            dst_ref=part_in.at[slot_, :, tile_at(n)],
            send_sem=rs_send.at[slot_, n],
            recv_sem=rs_recv.at[slot_, n],
            device_id=sum_peer(1 if slot_ < 3 else 3),
            device_id_type=MESH,
        )

    tiles = out_width // TILE

    @pl.loop(0, tiles)
    def _(n):
        cols = tile_at(n)
        wide = jnp.concatenate([rowf[...]] * (TILE // LANES), axis=1)
        gall[:, cols] = (wide * gall[:, cols].astype(F32)).astype(BF16)
        part_a[:, cols] = _dot(ht[chunk_rows(2, 0, chunk), :], gall[:, cols]).astype(BF16)
        rs_copy(0, n).start()
        rs_copy(3, n).start()

    @pl.loop(0, tiles)
    def _(n):
        cols = tile_at(n)
        part_b[0, :, cols] = _dot(ht[chunk_rows(1, 1, hc), :], gall[:, cols]).astype(BF16)
        rs_copy(1, n).start()
        part_b[1, :, cols] = _dot(ht[chunk_rows(3, 0, hc), :], gall[:, cols]).astype(BF16)
        rs_copy(4, n).start()

    @pl.loop(0, tiles)
    def _(n):
        cols = tile_at(n)
        term = _dot(ht[chunk_rows(1, 0, hc), :], gall[:, cols])
        rs_copy(0, n).wait_recv()
        part_c[0, :, cols] = (term + part_in[0, :, cols].astype(F32)).astype(BF16)
        rs_copy(2, n).start()
        term = _dot(ht[chunk_rows(3, 1, hc), :], gall[:, cols])
        rs_copy(3, n).wait_recv()
        part_c[1, :, cols] = (term + part_in[3, :, cols].astype(F32)).astype(BF16)
        rs_copy(5, n).start()

    @pl.loop(0, tiles)
    def _(n):
        cols = tile_at(n)
        own[:, cols] = _dot(ht[chunk_rows(0, 0, chunk), :], gall[:, cols])

    scale = 1.0 / (EX_BLK * SIDE * SIDE)

    @pl.loop(0, tiles)
    def _(n):
        cols = tile_at(n)
        for slot_ in (1, 2, 4, 5):
            rs_copy(slot_, n).wait_recv()
        upper = own[0:hc, cols] + part_in[2, :, cols].astype(F32) + part_in[4, :, cols].astype(F32)
        lower = own[hc:chunk, cols] + part_in[1, :, cols].astype(F32) + part_in[5, :, cols].astype(F32)
        out[0:hc, cols] = (upper * scale).astype(BF16)
        out[hc:chunk, cols] = (lower * scale).astype(BF16)

    for copies in zc:
        for copy in copies:
            copy.wait_send()
    for copy in fhs + sq_copies + f_copies:
        copy.wait_send()

    @pl.loop(0, tiles)
    def _(n):
        for slot_ in range(6):
            rs_copy(slot_, n).wait_send()


def body(hidden, grad_out, gate_weights, routes, example_ids):
    tokens, _, width = hidden.shape
    out_width = grad_out.shape[1]
    rows = 3 * tokens
    slice_w = width // SIDE
    chunk = slice_w // SIDE
    hc = chunk // 2
    wide = out_width + LANES
    tiles = out_width // TILE
    small = jnp.stack(
        [
            routes.reshape(-1).astype(F32),
            gate_weights.reshape(-1),
            jnp.repeat(example_ids, 2).astype(F32),
        ]
    )
    vmem = pl.BlockSpec(memory_space=pltpu.VMEM)
    hbm = pl.BlockSpec(memory_space=pl.ANY)
    dma = pltpu.SemaphoreType.DMA
    update, norms = pl.pallas_call(
        kernel,
        out_shape=(
            jax.ShapeDtypeStruct((chunk, out_width), BF16),
            jax.ShapeDtypeStruct((1, EX_BLK), F32),
        ),
        in_specs=[vmem, hbm, hbm],
        out_specs=(vmem, vmem),
        scratch_shapes=[
            pltpu.VMEM((tokens, 2, width), BF16),
            pltpu.VMEM((2 * tokens, width), BF16),
            pltpu.VMEM((tokens, out_width), BF16),
            pltpu.VMEM((rows, wide), BF16),
            pltpu.VMEM((SIDE, rows, slice_w), BF16),
            pltpu.VMEM((SIDE * rows, wide), BF16),
            pltpu.VMEM((SIDE, rows, slice_w), BF16),
            pltpu.VMEM((SIDE - 1, rows, slice_w), BF16),
            pltpu.VMEM((slice_w, SIDE * rows), BF16),
            pltpu.VMEM((rows, 2 * tokens), BF16),
            pltpu.VMEM((rows, rows), F32),
            pltpu.VMEM((rows, rows), F32),
            pltpu.VMEM((SIDE * rows, LANES), F32),
            pltpu.VMEM((8, LANES), F32),
            pltpu.VMEM((EXPERTS - 1, 8, LANES), F32),
            pltpu.VMEM((8, LANES), F32),
            pltpu.VMEM((SIDE - 1, 8, LANES), F32),
            pltpu.VMEM((chunk, out_width), BF16),
            pltpu.VMEM((2, hc, out_width), BF16),
            pltpu.VMEM((2, hc, out_width), BF16),
            pltpu.VMEM((6, hc, out_width), BF16),
            pltpu.VMEM((chunk, out_width), F32),
            dma((2,)),
            dma((1 + SIDE, EXPERTS - 1)),
            dma((1 + SIDE, EXPERTS - 1)),
            dma((SIDE - 1,)),
            dma((SIDE - 1,)),
            dma((SIDE - 1,)),
            dma((SIDE - 1,)),
            dma((EXPERTS - 1,)),
            dma((EXPERTS - 1,)),
            dma((SIDE - 1,)),
            dma((SIDE - 1,)),
            dma((6, tiles)),
            dma((6, tiles)),
        ],
        compiler_params=pltpu.CompilerParams(
            collective_id=0, has_side_effects=True, vmem_limit_bytes=60 * 1024 * 1024
        ),
    )(small, hidden, grad_out)
    return update[None], norms.reshape(EX_BLK)


def solution(mesh):
    return jax.shard_map(
        body,
        mesh=mesh,
        in_specs=(
            P(("dp", "expert"), None, None),
            P(("dp", "expert"), None),
            P(("dp", "expert"), None),
            P(("dp", "expert"), None),
            P(("dp", "expert")),
        ),
        out_specs=(P("expert", "dp", None), P("dp")),
        check_vma=False,
    )
```

time: 353 us -> 142 us (0.40)
  waiting for transfers between devices: 240 us -> 0 us
  Pallas kernels: 0 us -> 134 us
  matrix products: 31.1 us -> 0 us
  local copies, waits for them, and re-layouts: 27.4 us -> 4.86 us
  starting transfers between devices: 16.1 us -> 0 us
  between operations: 14.1 us -> 0.66 us
  blocking collectives: 12.6 us -> 0 us
  other arithmetic: 10.6 us -> 1.95 us
    reduce_scatter x1 -> x0, waiting for transfers between devices: 174 us -> none  [body(): lax.psum_scatter(lax.dot_general(hidden_in, clipped, (((0,), (0,)), ((),...]
    pallas_call x0 -> x1, Pallas kernels: none -> 134 us  [body(): pl.pallas_call(kernel, out_shape=(jax.ShapeDtypeStruct((chunk, out_width)...]
    all_to_all x3 -> x0, waiting for transfers between devices: 65.9 us -> none  [the longest x1 54.6 us: body(): lax.all_to_all(hidden_sent.reshape(experts, capacity, hidden_width), 'exp...]
    dot_general x3 -> x0, matrix products: 31.1 us -> none  [the longest x1 22 us: body(): lax.dot_general(hidden_in, clipped, (((0,), (0,)), ((), ())), preferred_e...]
    all_to_all x3 -> x0, starting transfers between devices: 16.1 us -> none  [the longest x1 6.81 us: body(): lax.all_to_all(owner_sent.reshape(experts, capacity), 'expert', split_axi...]
    psum x1 -> x0, blocking collectives: 12.6 us -> none  [body(): squares = lax.psum(square_part, 'expert')]
    scatter x2 -> x0, local copies, waits for them, and re-layouts: 11.5 us -> none  [the longest x1 10.1 us: body(): hidden_sent = jnp.zeros((experts * capacity, hidden_width), jnp.bfloat16)...]
    reshape x2 -> x0, local copies, waits for them, and re-layouts: 8.54 us -> none  [the longest x1 8.4 us: body(): hidden.reshape(-1, hidden_width)]
  transfers between devices with their start and end apart: 4 -> 0, of which waited for: 3 -> 0; matrix products, arithmetic and copies ran while one was open for 10% -> 0% of each run, Pallas kernels for 0% -> 0%
where the time goes in v1:
time: 142 us
  Pallas kernels  134 us (94%)
  local copies, waits for them, and re-layouts  4.86 us (3%)
  other arithmetic  1.95 us (1%)
    pallas_call x1, Pallas kernels, body(): pl.pallas_call(kernel, out_shape=(jax.ShapeDtypeStruct((chunk, out_width)...  134 us
    unnamed x5, local copies, waits for them, and re-layouts  4.24 us

profile of v1, /device:TPU:1, one launch (start us, length us, event | category | flops | bytes accessed | tf_op | source)
XLA Modules:
  0.0 141.9 jit_solution(1483073646230094023)
XLA Ops:
  0.6 0.7 convert_element_type.29
  1.3 0.7 convert_element_type.27
  2.0 0.1 copy.9
  2.1 0.1 convert_element_type.28
  2.2 0.1 broadcast_in_dim.6
  2.3 0.2 convert_element_type.30
  2.5 0.8 copy.10
  3.2 0.1 stack_reshape.3
  3.4 0.6 pad_maximum_fusion.small
  4.0 134.4 %shard_map.68 = (bf16[448,2048]{1,0:T(8,128)(2,1)}, f32[1,8]{1,0:T(1,128)}) custom-call(f32[3,256]{1,0:T(4,128)} %pad_maximum_fusion.small, bf16[128,2,7168]{2,1,0:T(2,128)(2,1)} %hid.1, bf16[128,2048]{1,0:T(8,128)(2,1)} %grad.1), custom_call_target="tpu_custom_call" | custom-call | tf_op jit(solution)/shard_map/pallas_call | solution.py:383
  138.4 0.0 copy-start
  138.4 2.9 %copy.13 = bf16[1,448,2048]{2,1,0:T(8,128)(2,1)} copy(bf16[1,448,2048]{2,1,0:T(8,128)(2,1)} %bitcast.2) | data formatting | bytes 3670016
  141.4 0.0 copy-done
  141.4 0.5 copy.14
Async XLA Ops:
  138.4 3.0 %copy-start = (f32[1,8]{1,0:T(1,128)S(1)}, f32[1,8]{1,0:T(1,128)}, u32[]{:S(2)}) copy-start(f32[1,8]{1,0:T(1,128)} %get-tuple-element.5) | copy-start | bytes 100

commit v2 on v1

--- a/solution.py
+++ b/solution.py
@@ -26,7 +26,7 @@
 
 
 def kernel(
-    small, hid, grad, out, norm_out,
+    routes, gates, ids, hid, grad, out, norm_out,
     hv, hp, gv, gs, hs, gall, hin, hg, ht, oh, hgram, mgram, rowf,
     sq_send, sq_recv, f_send, f_recv, part_a, part_b, part_c, part_in, own,
     in_sem, z_send, z_recv, fg_send, fg_recv, fh_send, fh_recv,
@@ -40,6 +40,7 @@
     slice_w = width // SIDE
     chunk = slice_w // SIDE
     hc = chunk // 2
+    g_cols = ((0, out_width // 2), (out_width // 2, out_width + LANES))
     threshold = math.sqrt(width * out_width * tokens * (0.43 + 0.01 * tokens))
 
     dp, ex = lax.axis_index("dp"), lax.axis_index("expert")
@@ -84,11 +85,12 @@
         pl.semaphore_signal(barrier, inc=1, device_id=peer, device_id_type=MESH)
 
     pairs = 2 * tokens
-    route = small[0:1, :]
-    gate = small[1:2, :]
-    local_id = small[2:3, :] - (dp * EX_BLK).astype(F32)
+    route = jnp.concatenate([routes[0:1, :], routes[1:2, :]], axis=1)
+    gate = jnp.concatenate([gates[0:1, :], gates[1:2, :]], axis=1)
+    local_id = (ids[0:1, :] - dp * EX_BLK).astype(F32)
+    local_id = jnp.concatenate([local_id, local_id], axis=1)
     expert_of = lax.broadcasted_iota(jnp.int32, (EXPERTS, pairs), 0)
-    chosen = route == expert_of.astype(F32)
+    chosen = route == expert_of
     before = lax.broadcasted_iota(jnp.int32, (pairs, pairs), 0) < lax.broadcasted_iota(
         jnp.int32, (pairs, pairs), 1
     )
@@ -98,24 +100,17 @@
     base = (lax.rem(expert_of, 2) * half + lax.div(expert_of, 2) * cap).astype(F32)
     slot = jnp.sum(jnp.where(chosen, base + place, 0.0), axis=0, keepdims=True)
     hit = slot == lax.broadcasted_iota(jnp.int32, (rows, pairs), 0).astype(F32)
-    onehot = jnp.where(hit, 1.0, 0.0).astype(BF16)
-    oh[...] = onehot
-    to_token = jnp.where(
-        lax.div(lax.broadcasted_iota(jnp.int32, (pairs, tokens), 0), 2)
-        == lax.broadcasted_iota(jnp.int32, (pairs, tokens), 1),
-        1.0,
-        0.0,
-    ).astype(BF16)
-    token_hot = _dot(onehot, to_token).astype(BF16)
+    hot = jnp.where(hit, 1.0, 0.0)
+    token_hot = (hot[:, 0:tokens] + hot[:, tokens:]).astype(BF16)
     slot_gate = jnp.sum(jnp.where(hit, gate, 0.0), axis=1, keepdims=True)
-    slot_id = jnp.sum(jnp.where(hit, local_id + 1.0, 0.0), axis=1, keepdims=True) - 1.0
-    lane = lax.broadcasted_iota(jnp.int32, (rows, LANES), 1).astype(F32)
-    gs[:, out_width:] = jnp.where(slot_id == lane, 1.0, 0.0).astype(BF16)
+
+    def pack_grads(first, last):
+        for n in range(first // TILE, last // TILE):
+            cols = slice(n * TILE, (n + 1) * TILE)
+            gs[:, cols] = (slot_gate * _dot(token_hot, gv[:, cols])).astype(BF16)
+
     g_in.wait()
-    for n in range(out_width // TILE):
-        cols = slice(n * TILE, (n + 1) * TILE)
-        gs[:, cols] = (slot_gate * _dot(token_hot, gv[:, cols])).astype(BF16)
-
+    pack_grads(*g_cols[0])
     pl.semaphore_wait(barrier, len(peers))
 
     my_rows = pl.ds(pl.multiple_of(ex * cap, 16), cap)
@@ -128,10 +123,11 @@
         copies = []
         for i, (dz, dc) in enumerate(zsteps):
             pz, pc = z_peer(dz, dc)
-            if k == 0:
-                src, dst = gs.at[block(pz, pc)], gall.at[my_grad_rows]
+            if k < 2:
+                cols = slice(*g_cols[k])
+                src, dst = gs.at[block(pz, pc), cols], gall.at[my_grad_rows, cols]
             else:
-                src, dst = hs.at[k - 1, block(pz, pc)], hin.at[k - 1, my_rows]
+                src, dst = hs.at[k - 2, block(pz, pc)], hin.at[k - 2, my_rows]
             copies.append(
                 pltpu.make_async_remote_copy(
                     src_ref=src,
@@ -144,10 +140,24 @@
             )
         return copies
 
-    zc = [z_copies(k) for k in range(1 + SIDE)]
+    zc = [z_copies(k) for k in range(2 + SIDE)]
     for copy in zc[0]:
         copy.start()
+
+    pack_grads(*g_cols[1])
+    slot_id = jnp.sum(jnp.where(hit, local_id + 1.0, 0.0), axis=1, keepdims=True) - 1.0
+    lane = lax.broadcasted_iota(jnp.int32, (rows, LANES), 1).astype(F32)
+    gs[:, out_width:] = jnp.where(slot_id == lane, 1.0, 0.0).astype(BF16)
+    for copy in zc[1]:
+        copy.start()
     gall[my_grad_rows, :] = gs[block(z, c), :]
+
+    from_pair = lax.broadcasted_iota(jnp.int32, (pairs, pairs), 0)
+    to_pair = lax.broadcasted_iota(jnp.int32, (pairs, pairs), 1)
+    interleave = 2 * lax.rem(from_pair, tokens) + lax.div(from_pair, tokens) == to_pair
+    oh[...] = _dot(
+        hot.astype(BF16), jnp.where(interleave, 1.0, 0.0).astype(BF16)
+    ).astype(BF16)
 
     h_in.wait()
     for j in range(SIDE):
@@ -171,12 +181,13 @@
             oh[half:rows, :], hv[:, :, jo].reshape(pairs, slice_w)
         ).astype(BF16)
 
-    def forward_grads(d):
+    def forward_grads(k, d):
+        cols = slice(*g_cols[k])
         return pltpu.make_async_remote_copy(
-            src_ref=gall.at[3 * rows : 4 * rows],
-            dst_ref=gall.at[(d - 1) * rows : d * rows],
-            send_sem=fg_send.at[d - 1],
-            recv_sem=fg_recv.at[d - 1],
+            src_ref=gall.at[3 * rows : 4 * rows, cols],
+            dst_ref=gall.at[(d - 1) * rows : d * rows, cols],
+            send_sem=fg_send.at[k, d - 1],
+            recv_sem=fg_recv.at[k, d - 1],
             device_id=gather_peer(d),
             device_id_type=MESH,
         )
@@ -191,31 +202,33 @@
             device_id_type=MESH,
         )
 
-    fgs = [forward_grads(d) for d in (1, 2, 3)]
+    fgs = [[forward_grads(k, d) for d in (1, 2, 3)] for k in range(2)]
     fhs = [forward_hidden(q) for q in range(SIDE - 1)]
 
-    for k in range(1 + SIDE):
-        if k < SIDE:
-            pack(k)
+    for k in range(2 + SIDE):
+        q = k - 2
+        if 1 <= k < 1 + SIDE:
+            pack(q + 1)
             for copy in zc[k + 1]:
                 copy.start()
-            hin[k, my_rows, :] = hs[k, block(z, c), :]
+            hin[q + 1, my_rows, :] = hs[q + 1, block(z, c), :]
         for copy in zc[k]:
             copy.wait_recv()
-        if k == 0:
-            for copy in fgs:
+        if k < 2:
+            for copy in fgs[k]:
                 copy.start()
-            g = gall[3 * rows : 4 * rows, 0:out_width]
-            b = gall[3 * rows : 4 * rows, out_width:]
-            mgram[...] = _dot_t(g, g) * _dot_t(b, b)
+            if k == 1:
+                g = gall[3 * rows : 4 * rows, 0:out_width]
+                b = gall[3 * rows : 4 * rows, out_width:]
+                mgram[...] = _dot_t(g, g) * _dot_t(b, b)
         else:
-            if k < SIDE:
-                fhs[k - 1].start()
-            h = hin[k - 1]
+            if q < SIDE - 1:
+                fhs[q].start()
+            h = hin[q]
             gram = _dot_t(h, h)
-            if k > 1:
+            if q > 0:
                 gram = gram + hgram[...]
-            if k < SIDE:
+            if q < SIDE - 1:
                 hgram[...] = gram
             else:
                 row_sums = jnp.sum(gram * mgram[...], axis=1, keepdims=True)
@@ -263,7 +276,7 @@
     for q in range(SIDE - 1):
         fhs[q].wait_recv()
         ht[:, q * rows : (q + 1) * rows] = hg[q].T
-    for copy in fgs:
+    for copy in fgs[0] + fgs[1]:
         copy.wait_recv()
         copy.wait_send()
     for copy in f_copies:
@@ -370,13 +383,6 @@
     hc = chunk // 2
     wide = out_width + LANES
     tiles = out_width // TILE
-    small = jnp.stack(
-        [
-            routes.reshape(-1).astype(F32),
-            gate_weights.reshape(-1),
-            jnp.repeat(example_ids, 2).astype(F32),
-        ]
-    )
     vmem = pl.BlockSpec(memory_space=pltpu.VMEM)
     hbm = pl.BlockSpec(memory_space=pl.ANY)
     dma = pltpu.SemaphoreType.DMA
@@ -386,7 +392,7 @@
             jax.ShapeDtypeStruct((chunk, out_width), BF16),
             jax.ShapeDtypeStruct((1, EX_BLK), F32),
         ),
-        in_specs=[vmem, hbm, hbm],
+        in_specs=[vmem, vmem, vmem, hbm, hbm],
         out_specs=(vmem, vmem),
         scratch_shapes=[
             pltpu.VMEM((tokens, 2, width), BF16),
@@ -412,10 +418,10 @@
             pltpu.VMEM((6, hc, out_width), BF16),
             pltpu.VMEM((chunk, out_width), F32),
             dma((2,)),
-            dma((1 + SIDE, EXPERTS - 1)),
-            dma((1 + SIDE, EXPERTS - 1)),
-            dma((SIDE - 1,)),
-            dma((SIDE - 1,)),
+            dma((2 + SIDE, EXPERTS - 1)),
+            dma((2 + SIDE, EXPERTS - 1)),
+            dma((2, SIDE - 1)),
+            dma((2, SIDE - 1)),
             dma((SIDE - 1,)),
             dma((SIDE - 1,)),
             dma((EXPERTS - 1,)),
@@ -428,7 +434,7 @@
         compiler_params=pltpu.CompilerParams(
             collective_id=0, has_side_effects=True, vmem_limit_bytes=60 * 1024 * 1024
         ),
-    )(small, hidden, grad_out)
+    )(routes.T, gate_weights.T, example_ids[None], hidden, grad_out)
     return update[None], norms.reshape(EX_BLK)
 
 

time: 142 us -> 135 us (0.951)
  Pallas kernels: 134 us -> 131 us
  other arithmetic: 1.95 us -> 0 us
    pallas_call x1, Pallas kernels: 134 us -> 131 us  [body(): pl.pallas_call(kernel, out_shape=(jax.ShapeDtypeStruct((chunk, out_width)...]
    unnamed x5 -> x4, local copies, waits for them, and re-layouts: 4.24 us -> 3.45 us
where the time goes in v2:
time: 135 us
  Pallas kernels  131 us (97%)
  local copies, waits for them, and re-layouts  3.45 us (3%)
    pallas_call x1, Pallas kernels, body(): pl.pallas_call(kernel, out_shape=(jax.ShapeDtypeStruct((chunk, out_width)...  131 us
    unnamed x4, local copies, waits for them, and re-layouts  3.45 us

profile of v2, /device:TPU:1, one launch (start us, length us, event | category | flops | bytes accessed | tf_op | source)
XLA Modules:
  0.0 135.0 jit_solution(14095381715436527302)
XLA Ops:
  0.6 130.8 %shard_map.68 = (bf16[448,2048]{1,0:T(8,128)(2,1)}, f32[1,8]{1,0:T(1,128)}) custom-call(s32[2,128]{1,0:T(2,128)} %bitcast.6, f32[2,128]{1,0:T(2,128)} %bitcast.7, s32[1,128]{1,0:T(1,128)} %bitcast.8, bf16[128,2,7168]{2,1,0:T(2,128)(2,1)} %hid.1, bf16[128,2048]{1,0:T(8,128)(2,1)} %grad.1), custom_call_target="tpu_custom_call" | custom-call | tf_op jit(solution)/shard_map/pallas_call | solution.py:389
  131.5 0.0 copy-start
  131.5 2.9 %copy.9 = bf16[1,448,2048]{2,1,0:T(8,128)(2,1)} copy(bf16[1,448,2048]{2,1,0:T(8,128)(2,1)} %bitcast.5) | data formatting | bytes 3670016
  134.4 0.0 copy-done
  134.4 0.5 copy.10
Async XLA Ops:
  131.5 3.0 %copy-start = (f32[1,8]{1,0:T(1,128)S(1)}, f32[1,8]{1,0:T(1,128)}, u32[]{:S(2)}) copy-start(f32[1,8]{1,0:T(1,128)} %get-tuple-element.5) | copy-start | bytes 100

commit v3 on v2

--- a/solution.py
+++ b/solution.py
@@ -389,8 +389,8 @@
     update, norms = pl.pallas_call(
         kernel,
         out_shape=(
-            jax.ShapeDtypeStruct((chunk, out_width), BF16),
-            jax.ShapeDtypeStruct((1, EX_BLK), F32),
+            pltpu.VMEM((chunk, out_width), BF16),
+            pltpu.VMEM((1, EX_BLK), F32),
         ),
         in_specs=[vmem, vmem, vmem, hbm, hbm],
         out_specs=(vmem, vmem),
@@ -432,7 +432,7 @@
             dma((6, tiles)),
         ],
         compiler_params=pltpu.CompilerParams(
-            collective_id=0, has_side_effects=True, vmem_limit_bytes=60 * 1024 * 1024
+            collective_id=0, has_side_effects=True, vmem_limit_bytes=54 * 1024 * 1024
         ),
     )(routes.T, gate_weights.T, example_ids[None], hidden, grad_out)
     return update[None], norms.reshape(EX_BLK)

time: 135 us -> 132 us (0.978)
  local copies, waits for them, and re-layouts: 3.45 us -> 1.74 us
    unnamed x4 -> x2, local copies, waits for them, and re-layouts: 3.45 us -> 1.74 us
where the time goes in v3:
time: 132 us
  Pallas kernels  130 us (98%)
  local copies, waits for them, and re-layouts  1.74 us (1%)
    pallas_call x1, Pallas kernels, body(): pl.pallas_call(kernel, out_shape=(pltpu.VMEM((chunk, out_width), BF16), p...  130 us

profile of v3, /device:TPU:1, one launch (start us, length us, event | category | flops | bytes accessed | tf_op | source)
XLA Modules:
  0.0 132.0 jit_solution(4392289052559006186)
XLA Ops:
  0.6 129.6 %shard_map.68 = (bf16[448,2048]{1,0:T(8,128)(2,1)S(1)}, f32[1,8]{1,0:T(1,128)S(1)}) custom-call(s32[2,128]{1,0:T(2,128)} %bitcast.7, f32[2,128]{1,0:T(2,128)} %bitcast.8, s32[1,128]{1,0:T(1,128)} %bitcast.9, bf16[128,2,7168]{2,1,0:T(2,128)(2,1)} %hid.1, bf16[128,2048]{1,0:T(8,128)(2,1)} %grad.1), custom_call_target="tpu_custom_call" | custom-call | tf_op jit(solution)/shard_map/pallas_call | solution.py:389
  130.2 1.2 copy.9
  131.4 0.5 copy.10

commit v4 on v3

--- a/solution.py
+++ b/solution.py
@@ -14,7 +14,7 @@
 EXPERTS = 8
 EX_BLK = 8
 LANES = 128
-TILE = 512
+TILE = 256
 
 
 def _dot(a, b):
@@ -28,9 +28,9 @@
 def kernel(
     routes, gates, ids, hid, grad, out, norm_out,
     hv, hp, gv, gs, hs, gall, hin, hg, ht, oh, hgram, mgram, rowf,
-    sq_send, sq_recv, f_send, f_recv, part_a, part_b, part_c, part_in, own,
+    sq_send, sq_recv, part_a, part_b, part_c, part_in, own,
     in_sem, z_send, z_recv, fg_send, fg_recv, fh_send, fh_recv,
-    sq_ssem, sq_rsem, f_ssem, f_rsem, rs_send, rs_recv,
+    sq_ssem, sq_rsem, rs_send, rs_recv,
 ):
     tokens, _, width = hid.shape
     out_width = grad.shape[1]
@@ -41,6 +41,9 @@
     chunk = slice_w // SIDE
     hc = chunk // 2
     g_cols = ((0, out_width // 2), (out_width // 2, out_width + LANES))
+    half_w = slice_w // 2
+    order = [(0, 0), (2, 0), (1, 0), (0, 1), (2, 1), (1, 1), (3, 0), (3, 1)]
+    n_pieces = 2 + len(order)
     threshold = math.sqrt(width * out_width * tokens * (0.43 + 0.01 * tokens))
 
     dp, ex = lax.axis_index("dp"), lax.axis_index("expert")
@@ -127,7 +130,8 @@
                 cols = slice(*g_cols[k])
                 src, dst = gs.at[block(pz, pc), cols], gall.at[my_grad_rows, cols]
             else:
-                src, dst = hs.at[k - 2, block(pz, pc)], hin.at[k - 2, my_rows]
+                at = order[k - 2]
+                src, dst = hs.at[(*at, block(pz, pc))], hin.at[(*at, my_rows)]
             copies.append(
                 pltpu.make_async_remote_copy(
                     src_ref=src,
@@ -140,7 +144,7 @@
             )
         return copies
 
-    zc = [z_copies(k) for k in range(2 + SIDE)]
+    zc = [z_copies(k) for k in range(n_pieces)]
     for copy in zc[0]:
         copy.start()
 
@@ -173,12 +177,13 @@
             at = j * slice_w + 2 * a * chunk
             hp[:, at : at + 2 * chunk] = pair
 
-    def pack(q):
-        je = pl.ds(pl.multiple_of(lax.rem(y + 1 + q, SIDE) * slice_w, LANES), slice_w)
-        jo = pl.ds(pl.multiple_of(lax.rem(x + 1 + q, SIDE) * slice_w, LANES), slice_w)
-        hs[q, 0:half, :] = _dot(oh[0:half, :], hp[:, je]).astype(BF16)
-        hs[q, half:rows, :] = _dot(
-            oh[half:rows, :], hv[:, :, jo].reshape(pairs, slice_w)
+    def pack(q, h):
+        je = lax.rem(y + 1 + q, SIDE) * slice_w + h * half_w
+        jo = lax.rem(x + 1 + q, SIDE) * slice_w + h * half_w
+        je, jo = (pl.ds(pl.multiple_of(j, LANES), half_w) for j in (je, jo))
+        hs[q, h, 0:half, :] = _dot(oh[0:half, :], hp[:, je]).astype(BF16)
+        hs[q, h, half:rows, :] = _dot(
+            oh[half:rows, :], hv[:, :, jo].reshape(pairs, half_w)
         ).astype(BF16)
 
     def forward_grads(k, d):
@@ -192,26 +197,34 @@
             device_id_type=MESH,
         )
 
-    def forward_hidden(q):
+    def forward_hidden(q, h):
         return pltpu.make_async_remote_copy(
-            src_ref=hin.at[q],
-            dst_ref=hg.at[q],
-            send_sem=fh_send.at[q],
-            recv_sem=fh_recv.at[q],
+            src_ref=hin.at[q, h],
+            dst_ref=hg.at[q, h],
+            send_sem=fh_send.at[q, h],
+            recv_sem=fh_recv.at[q, h],
             device_id=gather_peer(q + 1),
             device_id_type=MESH,
         )
 
     fgs = [[forward_grads(k, d) for d in (1, 2, 3)] for k in range(2)]
-    fhs = [forward_hidden(q) for q in range(SIDE - 1)]
-
-    for k in range(2 + SIDE):
-        q = k - 2
-        if 1 <= k < 1 + SIDE:
-            pack(q + 1)
+    fhs = [[forward_hidden(q, h) for h in range(2)] for q in range(SIDE - 1)]
+
+    def transpose(q, h, rows_in):
+        ht[h * half_w : (h + 1) * half_w, q * rows : (q + 1) * rows] = rows_in.T
+
+    def take(q, h):
+        fhs[q][h].wait_recv()
+        transpose(q, h, hg[q, h])
+
+    takes = {6: [(0, 0)], 7: [(2, 0), (1, 0)], 8: [(0, 1), (2, 1)]}
+    for k in range(n_pieces):
+        if 1 <= k < n_pieces - 1:
+            at = order[k - 1]
+            pack(*at)
             for copy in zc[k + 1]:
                 copy.start()
-            hin[q + 1, my_rows, :] = hs[q + 1, block(z, c), :]
+            hin[(*at, my_rows)] = hs[(*at, block(z, c))]
         for copy in zc[k]:
             copy.wait_recv()
         if k < 2:
@@ -222,68 +235,60 @@
                 b = gall[3 * rows : 4 * rows, out_width:]
                 mgram[...] = _dot_t(g, g) * _dot_t(b, b)
         else:
+            q, h = order[k - 2]
             if q < SIDE - 1:
-                fhs[q].start()
-            h = hin[q]
-            gram = _dot_t(h, h)
-            if q > 0:
+                fhs[q][h].start()
+            part = hin[q, h]
+            gram = _dot_t(part, part)
+            if k > 2:
                 gram = gram + hgram[...]
-            if q < SIDE - 1:
+            if k + 1 < n_pieces:
                 hgram[...] = gram
             else:
                 row_sums = jnp.sum(gram * mgram[...], axis=1, keepdims=True)
                 member = gall[3 * rows : 4 * rows, out_width:].astype(F32)
                 part = jnp.sum(row_sums * member, axis=0, keepdims=True)
                 sq_send[...] = jnp.broadcast_to(part, (8, LANES))
+            if q == SIDE - 1 and h == 0:
+                transpose(q, h, hin[q, h])
+            for at in takes.get(k, []):
+                take(*at)
 
     sq_copies = []
-    for i, (dz, dc) in enumerate(zsteps):
-        pz, pc = z_peer(dz, dc)
-        sq_copies.append(
-            pltpu.make_async_remote_copy(
-                src_ref=sq_send,
-                dst_ref=sq_recv.at[i],
-                send_sem=sq_ssem.at[i],
-                recv_sem=sq_rsem.at[i],
-                device_id=(dp, pz * 2 + pc),
-                device_id_type=MESH,
+    for d in (2, 1, 3, 0):
+        for i, (dz, dc) in enumerate(zsteps + [(0, 0)]):
+            if (d, dz, dc) == (0, 0, 0):
+                continue
+            pz, pc = z_peer(dz, dc)
+            sq_copies.append(
+                pltpu.make_async_remote_copy(
+                    src_ref=sq_send,
+                    dst_ref=sq_recv.at[d, i],
+                    send_sem=sq_ssem.at[d, i],
+                    recv_sem=sq_rsem.at[d, i],
+                    device_id=(along(d, pc)[0], pz * 2 + pc),
+                    device_id_type=MESH,
+                )
             )
-        )
     for copy in sq_copies:
         copy.start()
-    ht[:, 3 * rows : 4 * rows] = hin[SIDE - 1].T
-    total = sq_send[...]
-    for i, copy in enumerate(sq_copies):
-        copy.wait_recv()
-        total = total + sq_recv[i]
-    norms = jnp.sqrt(total)
-    norm_out[...] = norms[0:1, 0:EX_BLK] / threshold
-    f_send[...] = jnp.minimum(1.0, threshold / norms)
-    f_copies = []
-    for d in (1, 2, 3):
-        f_copies.append(
-            pltpu.make_async_remote_copy(
-                src_ref=f_send,
-                dst_ref=f_recv.at[d - 1],
-                send_sem=f_ssem.at[d - 1],
-                recv_sem=f_rsem.at[d - 1],
-                device_id=gather_peer(d),
-                device_id_type=MESH,
-            )
-        )
-    for copy in f_copies:
-        copy.start()
-    for q in range(SIDE - 1):
-        fhs[q].wait_recv()
-        ht[:, q * rows : (q + 1) * rows] = hg[q].T
+    transpose(3, 1, hin[SIDE - 1, 1])
+    take(1, 1)
     for copy in fgs[0] + fgs[1]:
         copy.wait_recv()
         copy.wait_send()
-    for copy in f_copies:
+    for copy in sq_copies:
         copy.wait_recv()
     for q in range(SIDE):
+        d = (q + 1) % SIDE
+        total = sq_send[...] if d == 0 else sq_recv[d, EXPERTS - 1]
+        for i in range(EXPERTS - 1):
+            total = total + sq_recv[d, i]
+        norms = jnp.sqrt(total)
+        if d == 0:
+            norm_out[...] = norms[0:1, 0:EX_BLK] / threshold
+        factors = jnp.minimum(1.0, threshold / norms)[0:1, :]
         span = slice(q * rows, (q + 1) * rows)
-        factors = f_send[0:1, :] if q == SIDE - 1 else f_recv[q, 0:1, :]
         row_factor = jnp.sum(
             gall[span, out_width:].astype(F32) * factors, axis=1, keepdims=True
         )
@@ -298,16 +303,16 @@
 
     def rs_copy(slot_, n):
         src = (
-            part_a.at[0:hc],
-            part_b.at[0],
-            part_c.at[0],
-            part_a.at[hc:chunk],
-            part_b.at[1],
-            part_c.at[1],
+            part_a.at[n, 0:hc],
+            part_b.at[0, n],
+            part_c.at[0, n],
+            part_a.at[n, hc:chunk],
+            part_b.at[1, n],
+            part_c.at[1, n],
         )[slot_]
         return pltpu.make_async_remote_copy(
-            src_ref=src.at[:, tile_at(n)],
-            dst_ref=part_in.at[slot_, :, tile_at(n)],
+            src_ref=src,
+            dst_ref=part_in.at[slot_, n],
             send_sem=rs_send.at[slot_, n],
             recv_sem=rs_recv.at[slot_, n],
             device_id=sum_peer(1 if slot_ < 3 else 3),
@@ -321,16 +326,16 @@
         cols = tile_at(n)
         wide = jnp.concatenate([rowf[...]] * (TILE // LANES), axis=1)
         gall[:, cols] = (wide * gall[:, cols].astype(F32)).astype(BF16)
-        part_a[:, cols] = _dot(ht[chunk_rows(2, 0, chunk), :], gall[:, cols]).astype(BF16)
+        part_a[n] = _dot(ht[chunk_rows(2, 0, chunk), :], gall[:, cols]).astype(BF16)
         rs_copy(0, n).start()
         rs_copy(3, n).start()
 
     @pl.loop(0, tiles)
     def _(n):
         cols = tile_at(n)
-        part_b[0, :, cols] = _dot(ht[chunk_rows(1, 1, hc), :], gall[:, cols]).astype(BF16)
+        part_b[0, n] = _dot(ht[chunk_rows(1, 1, hc), :], gall[:, cols]).astype(BF16)
         rs_copy(1, n).start()
-        part_b[1, :, cols] = _dot(ht[chunk_rows(3, 0, hc), :], gall[:, cols]).astype(BF16)
+        part_b[1, n] = _dot(ht[chunk_rows(3, 0, hc), :], gall[:, cols]).astype(BF16)
         rs_copy(4, n).start()
 
     @pl.loop(0, tiles)
@@ -338,11 +343,11 @@
         cols = tile_at(n)
         term = _dot(ht[chunk_rows(1, 0, hc), :], gall[:, cols])
         rs_copy(0, n).wait_recv()
-        part_c[0, :, cols] = (term + part_in[0, :, cols].astype(F32)).astype(BF16)
+        part_c[0, n] = (term + part_in[0, n].astype(F32)).astype(BF16)
         rs_copy(2, n).start()
         term = _dot(ht[chunk_rows(3, 1, hc), :], gall[:, cols])
         rs_copy(3, n).wait_recv()
-        part_c[1, :, cols] = (term + part_in[3, :, cols].astype(F32)).astype(BF16)
+        part_c[1, n] = (term + part_in[3, n].astype(F32)).astype(BF16)
         rs_copy(5, n).start()
 
     @pl.loop(0, tiles)
@@ -357,15 +362,15 @@
         cols = tile_at(n)
         for slot_ in (1, 2, 4, 5):
             rs_copy(slot_, n).wait_recv()
-        upper = own[0:hc, cols] + part_in[2, :, cols].astype(F32) + part_in[4, :, cols].astype(F32)
-        lower = own[hc:chunk, cols] + part_in[1, :, cols].astype(F32) + part_in[5, :, cols].astype(F32)
+        upper = own[0:hc, cols] + part_in[2, n].astype(F32) + part_in[4, n].astype(F32)
+        lower = own[hc:chunk, cols] + part_in[1, n].astype(F32) + part_in[5, n].astype(F32)
         out[0:hc, cols] = (upper * scale).astype(BF16)
         out[hc:chunk, cols] = (lower * scale).astype(BF16)
 
     for copies in zc:
         for copy in copies:
             copy.wait_send()
-    for copy in fhs + sq_copies + f_copies:
+    for copy in fhs[0] + fhs[1] + fhs[2] + sq_copies:
         copy.wait_send()
 
     @pl.loop(0, tiles)
@@ -399,40 +404,36 @@
             pltpu.VMEM((2 * tokens, width), BF16),
             pltpu.VMEM((tokens, out_width), BF16),
             pltpu.VMEM((rows, wide), BF16),
-            pltpu.VMEM((SIDE, rows, slice_w), BF16),
+            pltpu.VMEM((SIDE, 2, rows, slice_w // 2), BF16),
             pltpu.VMEM((SIDE * rows, wide), BF16),
-            pltpu.VMEM((SIDE, rows, slice_w), BF16),
-            pltpu.VMEM((SIDE - 1, rows, slice_w), BF16),
+            pltpu.VMEM((SIDE, 2, rows, slice_w // 2), BF16),
+            pltpu.VMEM((SIDE - 1, 2, rows, slice_w // 2), BF16),
             pltpu.VMEM((slice_w, SIDE * rows), BF16),
             pltpu.VMEM((rows, 2 * tokens), BF16),
             pltpu.VMEM((rows, rows), F32),
             pltpu.VMEM((rows, rows), F32),
             pltpu.VMEM((SIDE * rows, LANES), F32),
             pltpu.VMEM((8, LANES), F32),
-            pltpu.VMEM((EXPERTS - 1, 8, LANES), F32),
-            pltpu.VMEM((8, LANES), F32),
-            pltpu.VMEM((SIDE - 1, 8, LANES), F32),
-            pltpu.VMEM((chunk, out_width), BF16),
-            pltpu.VMEM((2, hc, out_width), BF16),
-            pltpu.VMEM((2, hc, out_width), BF16),
-            pltpu.VMEM((6, hc, out_width), BF16),
+            pltpu.VMEM((SIDE, EXPERTS, 8, LANES), F32),
+            pltpu.VMEM((tiles, chunk, TILE), BF16),
+            pltpu.VMEM((2, tiles, hc, TILE), BF16),
+            pltpu.VMEM((2, tiles, hc, TILE), BF16),
+            pltpu.VMEM((6, tiles, hc, TILE), BF16),
             pltpu.VMEM((chunk, out_width), F32),
             dma((2,)),
-            dma((2 + SIDE, EXPERTS - 1)),
-            dma((2 + SIDE, EXPERTS - 1)),
+            dma((2 + 2 * SIDE, EXPERTS - 1)),
+            dma((2 + 2 * SIDE, EXPERTS - 1)),
             dma((2, SIDE - 1)),
             dma((2, SIDE - 1)),
-            dma((SIDE - 1,)),
-            dma((SIDE - 1,)),
-            dma((EXPERTS - 1,)),
-            dma((EXPERTS - 1,)),
-            dma((SIDE - 1,)),
-            dma((SIDE - 1,)),
+            dma((SIDE - 1, 2)),
+            dma((SIDE - 1, 2)),
+            dma((SIDE, EXPERTS)),
+            dma((SIDE, EXPERTS)),
             dma((6, tiles)),
             dma((6, tiles)),
         ],
         compiler_params=pltpu.CompilerParams(
-            collective_id=0, has_side_effects=True, vmem_limit_bytes=54 * 1024 * 1024
+            collective_id=0, has_side_effects=True, vmem_limit_bytes=55 * 1024 * 1024
         ),
     )(routes.T, gate_weights.T, example_ids[None], hidden, grad_out)
     return update[None], norms.reshape(EX_BLK)

time: 132 us -> 131 us (level)
  no operation moved by 1% of the time
where the time goes in v4:
time: 131 us
  Pallas kernels  129 us (98%)
  local copies, waits for them, and re-layouts  1.74 us (1%)
    pallas_call x1, Pallas kernels, body(): pl.pallas_call(kernel, out_shape=(pltpu.VMEM((chunk, out_width), BF16), p...  129 us

profile of v4, /device:TPU:1, one launch (start us, length us, event | category | flops | bytes accessed | tf_op | source)
XLA Modules:
  0.0 131.4 jit_solution(7567066535703929846)
XLA Ops:
  0.6 129.0 %shard_map.68 = (bf16[448,2048]{1,0:T(8,128)(2,1)S(1)}, f32[1,8]{1,0:T(1,128)S(1)}) custom-call(s32[2,128]{1,0:T(2,128)} %bitcast.7, f32[2,128]{1,0:T(2,128)} %bitcast.8, s32[1,128]{1,0:T(1,128)} %bitcast.9, bf16[128,2,7168]{2,1,0:T(2,128)(2,1)} %hid.1, bf16[128,2048]{1,0:T(8,128)(2,1)} %grad.1), custom_call_target="tpu_custom_call" | custom-call | tf_op jit(solution)/shard_map/pallas_call | solution.py:394
  129.6 1.2 copy.9
  130.9 0.5 copy.10

commit v5 on v4

--- a/solution.py
+++ b/solution.py
@@ -26,11 +26,12 @@
 
 
 def kernel(
-    routes, gates, ids, hid, grad, out, norm_out,
+    routes_hbm, gates_hbm, ids_hbm, hid, grad, out, norm_out,
+    routes, gates, ids,
     hv, hp, gv, gs, hs, gall, hin, hg, ht, oh, hgram, mgram, rowf,
-    sq_send, sq_recv, part_a, part_b, part_c, part_in, own,
+    id_send, id_recv, sq_send, sq_recv, part_a, part_b, part_c, part_in, own,
     in_sem, z_send, z_recv, fg_send, fg_recv, fh_send, fh_recv,
-    sq_ssem, sq_rsem, rs_send, rs_recv,
+    id_ssem, id_rsem, sq_ssem, sq_rsem, rs_send, rs_recv,
 ):
     tokens, _, width = hid.shape
     out_width = grad.shape[1]
@@ -40,7 +41,7 @@
     slice_w = width // SIDE
     chunk = slice_w // SIDE
     hc = chunk // 2
-    g_cols = ((0, out_width // 2), (out_width // 2, out_width + LANES))
+    g_cols = ((0, out_width // 2), (out_width // 2, out_width))
     half_w = slice_w // 2
     order = [(0, 0), (2, 0), (1, 0), (0, 1), (2, 1), (1, 1), (3, 0), (3, 1)]
     n_pieces = 2 + len(order)
@@ -69,11 +70,6 @@
         pz = lax.rem(z + dz, SIDE)
         pc = c if dc == 0 else 1 - c
         return pz, pc
-
-    g_in = pltpu.make_async_copy(grad, gv, in_sem.at[0])
-    h_in = pltpu.make_async_copy(hid, hv, in_sem.at[1])
-    g_in.start()
-    h_in.start()
 
     barrier = pltpu.get_barrier_semaphore()
     peers = []
@@ -82,10 +78,20 @@
         peers.append((dp, pz * 2 + pc))
     for d in (1, 2, 3):
         peers.append(gather_peer(d))
-    for d in (1, 3):
-        peers.append(sum_peer(d))
     for peer in peers:
         pl.semaphore_signal(barrier, inc=1, device_id=peer, device_id_type=MESH)
+    small_in = [
+        pltpu.make_async_copy(src, dst, in_sem.at[2 + i])
+        for i, (src, dst) in enumerate(
+            [(routes_hbm, routes), (gates_hbm, gates), (ids_hbm, ids)]
+        )
+    ]
+    g_in = pltpu.make_async_copy(grad, gv, in_sem.at[0])
+    h_in = pltpu.make_async_copy(hid, hv, in_sem.at[1])
+    for copy in small_in + [g_in, h_in]:
+        copy.start()
+    for copy in small_in:
+        copy.wait()
 
     pairs = 2 * tokens
     route = jnp.concatenate([routes[0:1, :], routes[1:2, :]], axis=1)
@@ -106,6 +112,12 @@
     hot = jnp.where(hit, 1.0, 0.0)
     token_hot = (hot[:, 0:tokens] + hot[:, tokens:]).astype(BF16)
     slot_gate = jnp.sum(jnp.where(hit, gate, 0.0), axis=1, keepdims=True)
+    hot16 = hot.astype(BF16)
+    slot_id = _dot_t(jnp.broadcast_to(local_id + 1.0, (8, pairs)).astype(BF16), hot16)[0:1, :]
+    for j in range(EXPERTS):
+        id_send[j] = jnp.concatenate(
+            [slot_id[:, j * cap : (j + 1) * cap], jnp.zeros((1, LANES - cap), F32)], axis=1
+        )
 
     def pack_grads(first, last):
         for n in range(first // TILE, last // TILE):
@@ -144,23 +156,34 @@
             )
         return copies
 
+    id_copies = []
+    for i, (dz, dc) in enumerate(zsteps):
+        pz, pc = z_peer(dz, dc)
+        id_copies.append(
+            pltpu.make_async_remote_copy(
+                src_ref=id_send.at[pc * SIDE + pz],
+                dst_ref=id_recv.at[ex],
+                send_sem=id_ssem.at[i],
+                recv_sem=id_rsem.at[i],
+                device_id=(dp, pz * 2 + pc),
+                device_id_type=MESH,
+            )
+        )
     zc = [z_copies(k) for k in range(n_pieces)]
-    for copy in zc[0]:
+    for copy in zc[0] + id_copies:
         copy.start()
 
     pack_grads(*g_cols[1])
-    slot_id = jnp.sum(jnp.where(hit, local_id + 1.0, 0.0), axis=1, keepdims=True) - 1.0
-    lane = lax.broadcasted_iota(jnp.int32, (rows, LANES), 1).astype(F32)
-    gs[:, out_width:] = jnp.where(slot_id == lane, 1.0, 0.0).astype(BF16)
     for copy in zc[1]:
         copy.start()
-    gall[my_grad_rows, :] = gs[block(z, c), :]
+    gall[my_grad_rows, 0:out_width] = gs[block(z, c), :]
+    id_recv[ex] = id_send[c * SIDE + z]
 
     from_pair = lax.broadcasted_iota(jnp.int32, (pairs, pairs), 0)
     to_pair = lax.broadcasted_iota(jnp.int32, (pairs, pairs), 1)
     interleave = 2 * lax.rem(from_pair, tokens) + lax.div(from_pair, tokens) == to_pair
     oh[...] = _dot(
-        hot.astype(BF16), jnp.where(interleave, 1.0, 0.0).astype(BF16)
+        hot16, jnp.where(interleave, 1.0, 0.0).astype(BF16)
     ).astype(BF16)
 
     h_in.wait()
@@ -187,7 +210,7 @@
         ).astype(BF16)
 
     def forward_grads(k, d):
-        cols = slice(*g_cols[k])
+        cols = slice(g_cols[k][0], g_cols[k][1] + k * LANES)
         return pltpu.make_async_remote_copy(
             src_ref=gall.at[3 * rows : 4 * rows, cols],
             dst_ref=gall.at[(d - 1) * rows : d * rows, cols],
@@ -227,6 +250,13 @@
             hin[(*at, my_rows)] = hs[(*at, block(z, c))]
         for copy in zc[k]:
             copy.wait_recv()
+        if k == 1:
+            for copy in id_copies:
+                copy.wait_recv()
+            ids_in = jnp.concatenate([id_recv[e][:, 0:cap] for e in range(EXPERTS)], axis=1)
+            ids_in = jnp.broadcast_to(ids_in, (8, rows)).T[:, 0:1]
+            lane = lax.broadcasted_iota(jnp.int32, (rows, LANES), 1).astype(F32) + 1.0
+            gall[3 * rows : 4 * rows, out_width:] = jnp.where(ids_in == lane, 1.0, 0.0).astype(BF16)
         if k < 2:
             for copy in fgs[k]:
                 copy.start()
@@ -367,7 +397,7 @@
         out[0:hc, cols] = (upper * scale).astype(BF16)
         out[hc:chunk, cols] = (lower * scale).astype(BF16)
 
-    for copies in zc:
+    for copies in zc + [id_copies]:
         for copy in copies:
             copy.wait_send()
     for copy in fhs[0] + fhs[1] + fhs[2] + sq_copies:
@@ -397,13 +427,16 @@
             pltpu.VMEM((chunk, out_width), BF16),
             pltpu.VMEM((1, EX_BLK), F32),
         ),
-        in_specs=[vmem, vmem, vmem, hbm, hbm],
+        in_specs=[hbm] * 5,
         out_specs=(vmem, vmem),
         scratch_shapes=[
+            pltpu.VMEM((2, tokens), jnp.int32),
+            pltpu.VMEM((2, tokens), F32),
+            pltpu.VMEM((1, tokens), jnp.int32),
             pltpu.VMEM((tokens, 2, width), BF16),
             pltpu.VMEM((2 * tokens, width), BF16),
             pltpu.VMEM((tokens, out_width), BF16),
-            pltpu.VMEM((rows, wide), BF16),
+            pltpu.VMEM((rows, out_width), BF16),
             pltpu.VMEM((SIDE, 2, rows, slice_w // 2), BF16),
             pltpu.VMEM((SIDE * rows, wide), BF16),
             pltpu.VMEM((SIDE, 2, rows, slice_w // 2), BF16),
@@ -413,6 +446,8 @@
             pltpu.VMEM((rows, rows), F32),
             pltpu.VMEM((rows, rows), F32),
             pltpu.VMEM((SIDE * rows, LANES), F32),
+            pltpu.VMEM((EXPERTS, 1, LANES), F32),
+            pltpu.VMEM((EXPERTS, 1, LANES), F32),
             pltpu.VMEM((8, LANES), F32),
             pltpu.VMEM((SIDE, EXPERTS, 8, LANES), F32),
             pltpu.VMEM((tiles, chunk, TILE), BF16),
@@ -420,13 +455,15 @@
             pltpu.VMEM((2, tiles, hc, TILE), BF16),
             pltpu.VMEM((6, tiles, hc, TILE), BF16),
             pltpu.VMEM((chunk, out_width), F32),
-            dma((2,)),
+            dma((5,)),
             dma((2 + 2 * SIDE, EXPERTS - 1)),
             dma((2 + 2 * SIDE, EXPERTS - 1)),
             dma((2, SIDE - 1)),
             dma((2, SIDE - 1)),
             dma((SIDE - 1, 2)),
             dma((SIDE - 1, 2)),
+            dma((EXPERTS - 1,)),
+            dma((EXPERTS - 1,)),
             dma((SIDE, EXPERTS)),
             dma((SIDE, EXPERTS)),
             dma((6, tiles)),

time: 131 us -> 130 us (level)
    pallas_call x1, Pallas kernels: 129 us -> 128 us  [body(): pl.pallas_call(kernel, out_shape=(pltpu.VMEM((chunk, out_width), BF16), p...]
where the time goes in v5:
time: 130 us
  Pallas kernels  128 us (98%)
  local copies, waits for them, and re-layouts  1.74 us (1%)
    pallas_call x1, Pallas kernels, body(): pl.pallas_call(kernel, out_shape=(pltpu.VMEM((chunk, out_width), BF16), p...  128 us

profile of v5, /device:TPU:1, one launch (start us, length us, event | category | flops | bytes accessed | tf_op | source)
XLA Modules:
  0.0 130.0 jit_solution(10503942794085142960)
XLA Ops:
  0.6 127.6 %shard_map.68 = (bf16[448,2048]{1,0:T(8,128)(2,1)S(1)}, f32[1,8]{1,0:T(1,128)S(1)}) custom-call(s32[2,128]{1,0:T(2,128)} %bitcast.7, f32[2,128]{1,0:T(2,128)} %bitcast.8, s32[1,128]{1,0:T(1,128)} %bitcast.9, bf16[128,2,7168]{2,1,0:T(2,128)(2,1)} %hid.1, bf16[128,2048]{1,0:T(8,128)(2,1)} %grad.1), custom_call_target="tpu_custom_call" | custom-call | tf_op jit(solution)/shard_map/pallas_call | solution.py:424
  128.3 1.2 copy.9
  129.5 0.5 copy.10

commit v6 on v5

--- a/solution.py
+++ b/solution.py
@@ -239,6 +239,27 @@
     def take(q, h):
         fhs[q][h].wait_recv()
         transpose(q, h, hg[q, h])
+
+    n_sq = SIDE * EXPERTS - 1
+    sq_copies = []
+    for d in (2, 1, 3, 0):
+        for i, (dz, dc) in enumerate(zsteps + [(0, 0)]):
+            if (d, dz, dc) == (0, 0, 0):
+                continue
+            pz, pc = z_peer(dz, dc)
+            sq_copies.append(
+                pltpu.make_async_remote_copy(
+                    src_ref=sq_send,
+                    dst_ref=sq_recv.at[(d - 1) % SIDE * EXPERTS + i],
+                    send_sem=sq_ssem,
+                    recv_sem=sq_rsem,
+                    device_id=(along(d, pc)[0], pz * 2 + pc),
+                    device_id_type=MESH,
+                )
+            )
+
+    def sq_all(sem):
+        return pltpu.make_async_copy(sq_recv.at[0:n_sq], sq_recv.at[0:n_sq], sem)
 
     takes = {6: [(0, 0)], 7: [(2, 0), (1, 0)], 8: [(0, 1), (2, 1)]}
     for k in range(n_pieces):
@@ -278,28 +299,12 @@
                 row_sums = jnp.sum(gram * mgram[...], axis=1, keepdims=True)
                 member = gall[3 * rows : 4 * rows, out_width:].astype(F32)
                 part = jnp.sum(row_sums * member, axis=0, keepdims=True)
-                sq_send[...] = jnp.broadcast_to(part, (8, LANES))
+                sq_send[...] = part
             if q == SIDE - 1 and h == 0:
                 transpose(q, h, hin[q, h])
             for at in takes.get(k, []):
                 take(*at)
 
-    sq_copies = []
-    for d in (2, 1, 3, 0):
-        for i, (dz, dc) in enumerate(zsteps + [(0, 0)]):
-            if (d, dz, dc) == (0, 0, 0):
-                continue
-            pz, pc = z_peer(dz, dc)
-            sq_copies.append(
-                pltpu.make_async_remote_copy(
-                    src_ref=sq_send,
-                    dst_ref=sq_recv.at[d, i],
-                    send_sem=sq_ssem.at[d, i],
-                    recv_sem=sq_rsem.at[d, i],
-                    device_id=(along(d, pc)[0], pz * 2 + pc),
-                    device_id_type=MESH,
-                )
-            )
     for copy in sq_copies:
         copy.start()
     transpose(3, 1, hin[SIDE - 1, 1])
@@ -307,20 +312,15 @@
     for copy in fgs[0] + fgs[1]:
         copy.wait_recv()
         copy.wait_send()
-    for copy in sq_copies:
-        copy.wait_recv()
+    sq_recv[n_sq] = sq_send[...]
+    sq_all(sq_rsem).wait()
+    norms = jnp.sqrt(jnp.sum(sq_recv[...].reshape(SIDE, EXPERTS, LANES), axis=1))
+    norm_out[...] = norms[SIDE - 1 :, 0:EX_BLK] / threshold
+    factors = jnp.minimum(1.0, threshold / norms)
     for q in range(SIDE):
-        d = (q + 1) % SIDE
-        total = sq_send[...] if d == 0 else sq_recv[d, EXPERTS - 1]
-        for i in range(EXPERTS - 1):
-            total = total + sq_recv[d, i]
-        norms = jnp.sqrt(total)
-        if d == 0:
-            norm_out[...] = norms[0:1, 0:EX_BLK] / threshold
-        factors = jnp.minimum(1.0, threshold / norms)[0:1, :]
         span = slice(q * rows, (q + 1) * rows)
         row_factor = jnp.sum(
-            gall[span, out_width:].astype(F32) * factors, axis=1, keepdims=True
+            gall[span, out_width:].astype(F32) * factors[q : q + 1, :], axis=1, keepdims=True
         )
         rowf[span, :] = jnp.broadcast_to(row_factor, (rows, LANES))
 
@@ -400,8 +400,9 @@
     for copies in zc + [id_copies]:
         for copy in copies:
             copy.wait_send()
-    for copy in fhs[0] + fhs[1] + fhs[2] + sq_copies:
+    for copy in fhs[0] + fhs[1] + fhs[2]:
         copy.wait_send()
+    sq_all(sq_ssem).wait()
 
     @pl.loop(0, tiles)
     def _(n):
@@ -448,8 +449,8 @@
             pltpu.VMEM((SIDE * rows, LANES), F32),
             pltpu.VMEM((EXPERTS, 1, LANES), F32),
             pltpu.VMEM((EXPERTS, 1, LANES), F32),
-            pltpu.VMEM((8, LANES), F32),
-            pltpu.VMEM((SIDE, EXPERTS, 8, LANES), F32),
+            pltpu.VMEM((1, LANES), F32),
+            pltpu.VMEM((SIDE * EXPERTS, 1, LANES), F32),
             pltpu.VMEM((tiles, chunk, TILE), BF16),
             pltpu.VMEM((2, tiles, hc, TILE), BF16),
             pltpu.VMEM((2, tiles, hc, TILE), BF16),
@@ -464,8 +465,8 @@
             dma((SIDE - 1, 2)),
             dma((EXPERTS - 1,)),
             dma((EXPERTS - 1,)),
-            dma((SIDE, EXPERTS)),
-            dma((SIDE, EXPERTS)),
+            dma(()),
+            dma(()),
             dma((6, tiles)),
             dma((6, tiles)),
         ],

time: 130 us -> 129 us (level)
  no operation moved by 1% of the time
where the time goes in v6:
time: 129 us
  Pallas kernels  127 us (98%)
  local copies, waits for them, and re-layouts  1.74 us (1%)
    pallas_call x1, Pallas kernels, body(): pl.pallas_call(kernel, out_shape=(pltpu.VMEM((chunk, out_width), BF16), p...  127 us

profile of v6, /device:TPU:1, one launch (start us, length us, event | category | flops | bytes accessed | tf_op | source)
XLA Modules:
  0.0 129.2 jit_solution(5263015360235435138)
XLA Ops:
  0.6 126.8 %shard_map.68 = (bf16[448,2048]{1,0:T(8,128)(2,1)S(1)}, f32[1,8]{1,0:T(1,128)S(1)}) custom-call(s32[2,128]{1,0:T(2,128)} %bitcast.7, f32[2,128]{1,0:T(2,128)} %bitcast.8, s32[1,128]{1,0:T(1,128)} %bitcast.9, bf16[128,2,7168]{2,1,0:T(2,128)(2,1)} %hid.1, bf16[128,2048]{1,0:T(8,128)(2,1)} %grad.1), custom_call_target="tpu_custom_call" | custom-call | tf_op jit(solution)/shard_map/pallas_call | solution.py:425
  127.4 1.2 copy.9
  128.7 0.5 copy.10

commit v7 on v6

--- a/solution.py
+++ b/solution.py
@@ -29,7 +29,7 @@
     routes_hbm, gates_hbm, ids_hbm, hid, grad, out, norm_out,
     routes, gates, ids,
     hv, hp, gv, gs, hs, gall, hin, hg, ht, oh, hgram, mgram, rowf,
-    id_send, id_recv, sq_send, sq_recv, part_a, part_b, part_c, part_in, own,
+    id_send, id_recv, sq_send, sq_recv, factor_rows, part_a, part_b, part_c, part_in, own,
     in_sem, z_send, z_recv, fg_send, fg_recv, fh_send, fh_recv,
     id_ssem, id_rsem, sq_ssem, sq_rsem, rs_send, rs_recv,
 ):
@@ -234,11 +234,16 @@
     fhs = [[forward_hidden(q, h) for h in range(2)] for q in range(SIDE - 1)]
 
     def transpose(q, h, rows_in):
-        ht[h * half_w : (h + 1) * half_w, q * rows : (q + 1) * rows] = rows_in.T
+        @pl.loop(0, half_w // LANES)
+        def _(t):
+            at = pl.multiple_of(h * half_w + t * LANES, LANES)
+            ht[pl.ds(at, LANES), q * rows : (q + 1) * rows] = rows_in[
+                :, pl.ds(pl.multiple_of(t * LANES, LANES), LANES)
+            ].T
 
     def take(q, h):
         fhs[q][h].wait_recv()
-        transpose(q, h, hg[q, h])
+        transpose(q, h, hg.at[q, h])
 
     n_sq = SIDE * EXPERTS - 1
     sq_copies = []
@@ -301,13 +306,13 @@
                 part = jnp.sum(row_sums * member, axis=0, keepdims=True)
                 sq_send[...] = part
             if q == SIDE - 1 and h == 0:
-                transpose(q, h, hin[q, h])
+                transpose(q, h, hin.at[q, h])
             for at in takes.get(k, []):
                 take(*at)
 
     for copy in sq_copies:
         copy.start()
-    transpose(3, 1, hin[SIDE - 1, 1])
+    transpose(3, 1, hin.at[SIDE - 1, 1])
     take(1, 1)
     for copy in fgs[0] + fgs[1]:
         copy.wait_recv()
@@ -317,10 +322,13 @@
     norms = jnp.sqrt(jnp.sum(sq_recv[...].reshape(SIDE, EXPERTS, LANES), axis=1))
     norm_out[...] = norms[SIDE - 1 :, 0:EX_BLK] / threshold
     factors = jnp.minimum(1.0, threshold / norms)
-    for q in range(SIDE):
-        span = slice(q * rows, (q + 1) * rows)
+    factor_rows[...] = factors
+
+    @pl.loop(0, SIDE)
+    def _(q):
+        span = pl.ds(pl.multiple_of(q * rows, rows), rows)
         row_factor = jnp.sum(
-            gall[span, out_width:].astype(F32) * factors[q : q + 1, :], axis=1, keepdims=True
+            gall[span, out_width:].astype(F32) * factor_rows[pl.ds(q, 1), :], axis=1, keepdims=True
         )
         rowf[span, :] = jnp.broadcast_to(row_factor, (rows, LANES))
 
@@ -451,6 +459,7 @@
             pltpu.VMEM((EXPERTS, 1, LANES), F32),
             pltpu.VMEM((1, LANES), F32),
             pltpu.VMEM((SIDE * EXPERTS, 1, LANES), F32),
+            pltpu.VMEM((SIDE, LANES), F32),
             pltpu.VMEM((tiles, chunk, TILE), BF16),
             pltpu.VMEM((2, tiles, hc, TILE), BF16),
             pltpu.VMEM((2, tiles, hc, TILE), BF16),

time: 129 us -> 129 us (level)
  no operation moved by 1% of the time
where the time goes in v7:
time: 129 us
  Pallas kernels  127 us (98%)
  local copies, waits for them, and re-layouts  1.74 us (1%)
    pallas_call x1, Pallas kernels, body(): pl.pallas_call(kernel, out_shape=(pltpu.VMEM((chunk, out_width), BF16), p...  127 us

profile of v7, /device:TPU:1, one launch (start us, length us, event | category | flops | bytes accessed | tf_op | source)
XLA Modules:
  0.0 129.3 jit_solution(17249979191552306591)
XLA Ops:
  0.6 126.9 %shard_map.68 = (bf16[448,2048]{1,0:T(8,128)(2,1)S(1)}, f32[1,8]{1,0:T(1,128)S(1)}) custom-call(s32[2,128]{1,0:T(2,128)} %bitcast.7, f32[2,128]{1,0:T(2,128)} %bitcast.8, s32[1,128]{1,0:T(1,128)} %bitcast.9, bf16[128,2,7168]{2,1,0:T(2,128)(2,1)} %hid.1, bf16[128,2048]{1,0:T(8,128)(2,1)} %grad.1), custom_call_target="tpu_custom_call" | custom-call | tf_op jit(solution)/shard_map/pallas_call | solution.py:433
  127.5 1.2 copy.9
  128.7 0.5 copy.10

commit v8 on v7

--- a/solution.py
+++ b/solution.py
@@ -364,8 +364,9 @@
         cols = tile_at(n)
         wide = jnp.concatenate([rowf[...]] * (TILE // LANES), axis=1)
         gall[:, cols] = (wide * gall[:, cols].astype(F32)).astype(BF16)
-        part_a[n] = _dot(ht[chunk_rows(2, 0, chunk), :], gall[:, cols]).astype(BF16)
+        part_a[n, 0:hc] = _dot(ht[chunk_rows(2, 0, hc), :], gall[:, cols]).astype(BF16)
         rs_copy(0, n).start()
+        part_a[n, hc:chunk] = _dot(ht[chunk_rows(2, 1, hc), :], gall[:, cols]).astype(BF16)
         rs_copy(3, n).start()
 
     @pl.loop(0, tiles)

time: 129 us -> 129 us (level)
  no operation moved by 1% of the time
where the time goes in v8:
time: 129 us
  Pallas kernels  127 us (98%)
  local copies, waits for them, and re-layouts  1.74 us (1%)
    pallas_call x1, Pallas kernels, body(): pl.pallas_call(kernel, out_shape=(pltpu.VMEM((chunk, out_width), BF16), p...  127 us

profile of v8, /device:TPU:1, one launch (start us, length us, event | category | flops | bytes accessed | tf_op | source)
XLA Modules:
  0.0 129.2 jit_solution(10767022034820794383)
XLA Ops:
  0.6 126.8 %shard_map.68 = (bf16[448,2048]{1,0:T(8,128)(2,1)S(1)}, f32[1,8]{1,0:T(1,128)S(1)}) custom-call(s32[2,128]{1,0:T(2,128)} %bitcast.7, f32[2,128]{1,0:T(2,128)} %bitcast.8, s32[1,128]{1,0:T(1,128)} %bitcast.9, bf16[128,2,7168]{2,1,0:T(2,128)(2,1)} %hid.1, bf16[128,2048]{1,0:T(8,128)(2,1)} %grad.1), custom_call_target="tpu_custom_call" | custom-call | tf_op jit(solution)/shard_map/pallas_call | solution.py:434
  127.5 1.2 copy.9
  128.7 0.5 copy.10
